TPU v7x, 128 devices: a whole 4x4x4 slice. The times are simulated.
128 devices in a mesh: gx: 8 (over x, core), gy: 16 (over z, y).
Axes of the slice: x: 4, y: 4, z: 4, core: 2. Of those that a mesh axis runs over, the one named last changes fastest.
Arguments:
- feats: bfloat16 [64, 524288], P(None, ('gx', 'gy')), may hold values from -6 to 6
- face_rows: int32 [128, 4, 128], P(('gx', 'gy')), may hold values from 0 to 4095
- neighbours: int32 [27, 524288], P(None, ('gx', 'gy')), may hold values from -1 to 4607, as said below
- z_dest: int32 [2, 524288], P(None, ('gx', 'gy')), may hold values from 0 to 4095, as said below
- h_dest: int32 [2, 524288], P(None, ('gx', 'gy')), may hold values from 0 to 4095, as said below
- conv_weight: bfloat16 [27, 64, 64], replicated, may hold values from -0.15625 to 0.15625
- qkv_weight: bfloat16 [2, 64, 192], replicated, may hold values from -4 to 4
- out_weight: bfloat16 [2, 64, 64], replicated, may hold values from -0.75 to 0.75
- up_weight: bfloat16 [2, 64, 256], replicated, may hold values from -0.75 to 0.75
- down_weight: bfloat16 [2, 256, 64], replicated, may hold values from -0.375 to 0.375
- norm_gains: float32 [5, 64], replicated, may hold values from 0.1 to 1.9
Outputs:
- result: bfloat16 [64, 524288], P(None, ('gx', 'gy'))
Inputs may be any that keep to these rules, and one draw needn't show every extreme that they name: `neighbours`: entry 13 of each point is the point itself; other entries are -1 (no neighbour), a local point 0 to 4095, or 4096 + f * 128 + r for row r of the f-th block of face points in extended. `z_dest`: row 0 is the owner device, row 1 the slot in the owner's patch buffer; all (owner, slot) pairs are distinct, so every device owns 4096 points. The points of one device go 48 to each of half of the devices and a third of 48 to each of the other half. `h_dest`: same form and counts as z_dest, for the Hilbert order. `face_rows`: rows 0 to 3 list points of the tile's lower x, upper x, lower y and upper y faces.
All inputs are finite; a program needn't handle non-finite values.
Results may differ from a plain program's by a relative error of at most 0.019.
The roundings to bfloat16 on the way count: a program that leaves them out, or rounds other values in their place, can miss the bound.
Values may be sent and summed in bfloat16 or wider, within the bound.
No kernel may reach another device: no remote copies, remote signals or barrier semaphores. Data moves between devices by JAX's collectives and lax.ppermute only.
A program may use at most 128 MiB of HBM per device.

v0:
```python
import functools

import jax
import jax.numpy as jnp
from jax import lax
from jax.experimental import pallas as pl
from jax.experimental.pallas import tpu as pltpu
from jax.sharding import PartitionSpec as P

HEADS = 4
HEAD_DIM = 16
PATCH = 1024
C = 64
PTS = 4096
FACE = 128
EXT = PTS + 4 * FACE
TROWS = EXT + 8
DEV = 128
CAP = 48
HALF = CAP // 2
PACK = DEV * HALF
ON_CAP = 64
ON_HALF = ON_CAP // 2
EXTRA = 8
OUT_STRIDE = HALF + EXTRA
ON_STRIDE = ON_HALF + EXTRA
OUT_PACK = DEV * OUT_STRIDE
ON_PACK = DEV * ON_STRIDE
PAIRS = 13
BLK = 512
UN = 16
GROUP = 32
GROUPS = PTS // GROUP
LISTS = 4
LOG2_E = 1.4426950408889634
SAFE = 72.0
EPS = 1e-05
VMEM = 60 * 2**20
BF = jnp.bfloat16
F32 = jnp.float32


def lane_norm(values, gain):
    average = jnp.mean(values, axis=1, keepdims=True)
    centred = values - average
    spread = jnp.mean(centred * centred, axis=1, keepdims=True)
    return centred * lax.rsqrt(spread + EPS) * gain


def chan_norm(values, gain):
    average = jnp.mean(values, axis=0, keepdims=True)
    centred = values - average
    spread = jnp.mean(centred * centred, axis=0, keepdims=True)
    return centred * lax.rsqrt(spread + EPS) * gain


def low_lanes(rows):
    return lax.broadcasted_iota(jnp.int32, (rows, 128), 1) < C


def pack_rows(rows_ref, out_ref):
    count = out_ref.shape[0]

    def part(b, _):
        at = pl.multiple_of(b * 512, 512)
        low = rows_ref[pl.ds(at, 512), :]
        high = pltpu.roll(rows_ref[pl.ds(at + count, 512), :], C, 1)
        out_ref[pl.ds(at, 512), :] = jnp.where(low_lanes(512), low, high).astype(BF)
        return 0

    lax.fori_loop(0, count // 512, part, 0)


def unpack_rows(in_ref, rows_ref):
    count = in_ref.shape[0]

    def part(b, _):
        at = pl.multiple_of(b * 512, 512)
        both = in_ref[pl.ds(at, 512), :].astype(F32)
        rows_ref[pl.ds(at, 512), :] = both
        rows_ref[pl.ds(at + count, 512), :] = pltpu.roll(both, C, 1)
        return 0

    lax.fori_loop(0, count // 512, part, 0)


def move_rows(count, read, place_ref, rows_ref):
    def move(g, _):
        at = g * UN
        taken = [read(at + u) for u in range(UN)]
        for u in range(UN):
            rows_ref[pl.ds(place_ref[at + u], 1), :] = taken[u]
        return 0

    lax.fori_loop(0, count // UN, move, 0)


def put_codes(code_ref, rows_ref, half):
    def put(g, _):
        for u in range(8):
            d = g * 8 + u
            codes = code_ref[pl.ds(pl.multiple_of(d * EXTRA, EXTRA), EXTRA), :]
            at = pl.multiple_of(d * (half + EXTRA) + half, 8)
            rows_ref[pl.ds(at, EXTRA), :] = codes
        return 0

    lax.fori_loop(0, DEV // 8, put, 0)


def conv_kernel(
    near_ref, place_ref, code_ref, feats_ref, low_x, high_x, low_y, high_y, weight_ref, gain_ref,
    out_ref, *scratch,
):
    table, sums, rows, ext, orders = scratch[:5]
    lists, sems = scratch[5 : 5 + LISTS], scratch[5 + LISTS]

    def list_copy(g, b):
        return pltpu.make_async_copy(orders.at[g], lists[b], sems.at[b])

    offset = lax.broadcasted_iota(jnp.int32, (2 * PAIRS + 1, 128), 0)
    base = (offset - (offset > PAIRS).astype(jnp.int32)) // 2 * TROWS
    blank = jnp.zeros((32 - (2 * PAIRS + 1), 128), jnp.int32)
    for r in range(8):
        part = []
        for u in range(4 * r, 4 * r + 4):
            near = near_ref[:, u * 128 : (u + 1) * 128]
            part += [jnp.where(near < 0, EXT, near) + base, blank]
        orders[:, r, :] = jnp.concatenate(part, axis=0).T
    for b in range(LISTS):
        list_copy(b, b).start()

    def turn(b, _):
        at = pl.multiple_of(b * 512, 512)
        ext[pl.ds(at, 512), :] = feats_ref[:, pl.ds(at, 512)].astype(F32).T.astype(BF)
        return 0

    lax.fori_loop(0, PTS // 512, turn, 0)
    for i, face in enumerate((low_x, high_x, low_y, high_y)):
        ext[PTS + i * FACE : PTS + (i + 1) * FACE, :] = face[...].astype(F32).T.astype(BF)
    kept = [o for o in range(2 * PAIRS + 1) if o != PAIRS]
    pairs = [
        jnp.concatenate([weight_ref[kept[2 * j]], weight_ref[kept[2 * j + 1]]], axis=1)
        for j in range(PAIRS)
    ]

    def fill(b, _):
        at = pl.multiple_of(b * 512, 512)
        chunk = ext[pl.ds(at, 512), :]
        for j in range(PAIRS):
            table[pl.ds(pl.multiple_of(j * TROWS + at, 8), 512), :] = jnp.dot(
                chunk, pairs[j], preferred_element_type=F32
            )
        return 0

    lax.fori_loop(0, EXT // 512, fill, 0)
    for j in range(PAIRS):
        table[j * TROWS + EXT : (j + 1) * TROWS, :] = jnp.zeros((TROWS - EXT, 128), F32)

    low_row = low_lanes(1)

    def gather(step, _):
        for b in range(LISTS):
            g = step * LISTS + b
            list_copy(g, b).wait()
            for u in range(GROUP):
                even, odd = None, None
                for j in range(PAIRS):
                    at = u * 32 + kept[2 * j]
                    first = table[pl.ds(lists[b][at // 128, at % 128], 1), :]
                    at = u * 32 + kept[2 * j + 1]
                    second = table[pl.ds(lists[b][at // 128, at % 128], 1), :]
                    even = first if even is None else even + first
                    odd = second if odd is None else odd + second
                sums[pl.ds(u * GROUPS + g, 1), :] = jnp.where(low_row, even, odd)
            list_copy(jnp.minimum(g + LISTS, GROUPS - 1), b).start()
        return 0

    lax.fori_loop(0, GROUPS // LISTS, gather, 0)
    for b in range(LISTS):
        list_copy(GROUPS - 1, b).wait()

    def finish(b, _):
        at = pl.multiple_of(b * BLK, BLK)
        own = ext[pl.ds(at, BLK), :]
        both = sums[pl.ds(at, BLK), :]
        conv = both[:, :C] + both[:, C:] + jnp.dot(own, weight_ref[PAIRS], preferred_element_type=F32)
        sums[pl.ds(at, BLK), :C] = own.astype(F32) + lane_norm(conv, gain_ref[0:1, :])
        return 0

    lax.fori_loop(0, PTS // BLK, finish, 0)
    move_rows(PTS, lambda i: sums[pl.ds(i, 1), :], place_ref, rows)
    put_codes(code_ref, rows, HALF)
    pack_rows(rows, out_ref)


def conv_send(near, place, codes, feats, faces, weight, gains):
    return pl.pallas_call(
        conv_kernel,
        in_specs=[pl.BlockSpec(memory_space=pltpu.VMEM), pl.BlockSpec(memory_space=pltpu.SMEM)]
        + [pl.BlockSpec(memory_space=pltpu.VMEM)] * 8,
        out_specs=pl.BlockSpec(memory_space=pltpu.VMEM),
        out_shape=jax.ShapeDtypeStruct((OUT_PACK, 128), BF),
        scratch_shapes=[
            pltpu.VMEM((PAIRS * TROWS, 128), F32),
            pltpu.VMEM((PTS, 128), F32),
            pltpu.VMEM((2 * OUT_PACK, 128), F32),
            pltpu.VMEM((EXT, C), BF),
            pltpu.VMEM((GROUPS, 8, 128), jnp.int32),
        ]
        + [pltpu.SMEM((8, 128), jnp.int32)] * LISTS
        + [pltpu.SemaphoreType.DMA((LISTS,))],
        compiler_params=pltpu.CompilerParams(vmem_limit_bytes=VMEM),
        cost_estimate=pl.CostEstimate(flops=10**11, bytes_accessed=10**6, transcendentals=0),
        name="conv_send",
    )(near, place, codes, feats, *faces, weight, gains)


def relay_kernel(from_ref, to_ref, in_ref, out_ref, source, target):
    unpack_rows(in_ref, source)

    move_rows(PTS, lambda i: source[pl.ds(from_ref[i], 1), :], to_ref, target)
    pack_rows(target, out_ref)


def relay(place_from, place_to, packed):
    return pl.pallas_call(
        relay_kernel,
        in_specs=[
            pl.BlockSpec(memory_space=pltpu.SMEM),
            pl.BlockSpec(memory_space=pltpu.SMEM),
            pl.BlockSpec(memory_space=pltpu.VMEM),
        ],
        out_specs=pl.BlockSpec(memory_space=pltpu.VMEM),
        out_shape=jax.ShapeDtypeStruct((PACK, 128), BF),
        scratch_shapes=[
            pltpu.VMEM((2 * PACK, 128), F32),
            pltpu.VMEM((2 * PACK, 128), F32),
        ],
        compiler_params=pltpu.CompilerParams(vmem_limit_bytes=VMEM),
        cost_estimate=pl.CostEstimate(flops=10**9, bytes_accessed=10**6, transcendentals=0),
        name="relay",
    )(place_from, place_to, packed)


def turned_dot(weight, values):
    return lax.dot_general(
        weight, values, (((0,), (0,)), ((), ())), preferred_element_type=F32
    )


def patch_math(j, x, qkv_ref, outw_ref, up_ref, down_ref, gain_ref, mixed, values_ref):
    normed = chan_norm(x, gain_ref[:, 2 * j + 1 : 2 * j + 2]).astype(BF)
    qkv = turned_dot(qkv_ref[j], normed).astype(BF)
    queries = qkv[:C].astype(F32)
    keys = qkv[C : 2 * C].astype(F32)
    keys_t = keys.T
    head_of = lax.broadcasted_iota(jnp.int32, (C, PATCH), 0) // HEAD_DIM
    ones = jnp.ones((HEAD_DIM, PATCH), BF)

    def of_head(h, values):
        return jnp.where(head_of == h, values, 0.0)

    def weighted(values, weights):
        summed = jnp.dot(
            jnp.concatenate([values, ones], axis=0), weights, preferred_element_type=F32
        )
        return (summed[:HEAD_DIM] / summed[HEAD_DIM : HEAD_DIM + 1]).astype(BF)

    def longest(values):
        squares = (values * values).reshape(HEADS, HEAD_DIM, PATCH)
        return jnp.max(jnp.sum(squares, axis=1), axis=1, keepdims=True)

    reach = jnp.max(longest(queries) * longest(keys))
    safe = reach <= (SAFE * HEAD_DIM**0.5) ** 2

    @pl.when(safe)
    def _():
        scaled = queries * (HEAD_DIM**-0.5 * LOG2_E)
        upper = scaled.astype(BF).astype(F32)
        lower = scaled - upper
        keys_2 = jnp.concatenate([keys_t, keys_t], axis=1).astype(BF)
        for h in range(HEADS):
            split = jnp.concatenate([of_head(h, upper), of_head(h, lower)], axis=0).astype(BF)
            scores = jnp.dot(keys_2, split, preferred_element_type=F32)
            first = h * HEAD_DIM
            values = qkv[2 * C + first : 2 * C + first + HEAD_DIM]
            mixed[first : first + HEAD_DIM, :] = weighted(values, jnp.exp2(scores).astype(BF))

    @pl.when(jnp.logical_not(safe))
    def _():
        keys_1 = keys_t.astype(BF)
        values_ref[...] = qkv[2 * C :]

        def head(h, _):
            one_head = of_head(h, queries * HEAD_DIM**-0.5).astype(BF)
            scores = jnp.dot(keys_1, one_head, preferred_element_type=F32)
            weights = jnp.exp(scores - jnp.max(scores, axis=0, keepdims=True)).astype(BF)
            at = pl.ds(pl.multiple_of(h * HEAD_DIM, HEAD_DIM), HEAD_DIM)
            mixed[at, :] = weighted(values_ref[at, :], weights)
            return 0

        lax.fori_loop(0, HEADS, head, 0)

    residual = x + turned_dot(outw_ref[j], mixed[...])
    normed_b = chan_norm(residual, gain_ref[:, 2 * j + 2 : 2 * j + 3]).astype(BF)
    raised = turned_dot(up_ref[j], normed_b)
    hidden = (0.5 * raised * (1.0 + lax.erf(raised * 0.5**0.5))).astype(BF)
    return residual + turned_dot(down_ref[j], hidden)


def place_rows(half, slot_ref, in_ref, source, rows):
    unpack_rows(in_ref, source)
    count = in_ref.shape[0]
    stride = count // DEV

    def place(d, _):
        for side in range(2):
            at = side * count + d * stride
            taken = [source[pl.ds(at + k, 1), :] for k in range(half)]
            entry = d * 2 * half + side * half
            for k in range(half):
                rows[pl.ds(slot_ref[entry + k], 1), :] = taken[k]
        return 0

    lax.fori_loop(0, DEV, place, 0)


def first_kernel(
    slot_ref, onward_ref, in_ref, code_ref, qkv_ref, outw_ref, up_ref, down_ref, gain_ref,
    out_ref, done_ref, source, rows, mixed, values_ref,
):
    place_rows(HALF, slot_ref, in_ref, source, rows)
    done_ref[PTS:, :] = jnp.zeros((8, 128), F32)

    def patch(p, _):
        at = pl.multiple_of(p * PATCH, PATCH)
        x = rows[pl.ds(at, PATCH), :].T[:C]
        y = patch_math(0, x, qkv_ref, outw_ref, up_ref, down_ref, gain_ref, mixed, values_ref)
        y = y.astype(BF).astype(F32)
        done_ref[pl.ds(at, PATCH), :] = jnp.concatenate([y, y], axis=0).T
        return 0

    lax.fori_loop(0, PTS // PATCH, patch, 0)
    move_rows(DEV * CAP, lambda i: done_ref[pl.ds(slot_ref[i], 1), :], onward_ref, source)
    put_codes(code_ref, source, ON_HALF)
    pack_rows(source, out_ref)


def last_kernel(
    half, slot_ref, in_ref, qkv_ref, outw_ref, up_ref, down_ref, gain_ref,
    out_ref, source, rows, mixed, values_ref,
):
    place_rows(half, slot_ref, in_ref, source, rows)

    def patch(p, _):
        at = pl.multiple_of(p * PATCH, PATCH)
        x = rows[pl.ds(at, PATCH), :].T[:C]
        y = patch_math(1, x, qkv_ref, outw_ref, up_ref, down_ref, gain_ref, mixed, values_ref)
        out_ref[:, pl.ds(at, PATCH)] = y.astype(BF)
        return 0

    lax.fori_loop(0, PTS // PATCH, patch, 0)


def block_call(kernel, lists, operands, out_shape, buffer_rows, name):
    return pl.pallas_call(
        kernel,
        in_specs=[pl.BlockSpec(memory_space=pltpu.SMEM)] * len(lists)
        + [pl.BlockSpec(memory_space=pltpu.VMEM)] * len(operands),
        out_specs=jax.tree.map(lambda _: pl.BlockSpec(memory_space=pltpu.VMEM), out_shape),
        out_shape=out_shape,
        scratch_shapes=[
            pltpu.VMEM((buffer_rows, 128), F32),
            pltpu.VMEM((PTS + 8, 128), F32),
            pltpu.VMEM((C, PATCH), BF),
            pltpu.VMEM((C, PATCH), BF),
        ],
        compiler_params=pltpu.CompilerParams(vmem_limit_bytes=VMEM),
        cost_estimate=pl.CostEstimate(flops=4 * 10**10, bytes_accessed=10**6, transcendentals=0),
        name=name,
    )(*lists, *operands)


def first_block(slots, onward, packed, codes, weights):
    shapes = (
        jax.ShapeDtypeStruct((ON_PACK, 128), BF),
        jax.ShapeDtypeStruct((PTS + 8, 128), F32),
    )
    return block_call(
        first_kernel, (slots, onward), (packed, codes, *weights), shapes, 2 * ON_PACK + 8,
        "first_block",
    )


def last_block(half, slots, packed, weights):
    return block_call(
        functools.partial(last_kernel, half), (slots,), (packed, *weights),
        jax.ShapeDtypeStruct((C, PTS), BF), 2 * packed.shape[0], "last_block",
    )


def fetch_kernel(slot_ref, done_ref, out_ref, source):
    low_row = low_lanes(1)

    def fetch(g, _):
        at = g * UN
        taken = []
        for u in range(UN):
            low = done_ref[pl.ds(slot_ref[at + u], 1), :]
            high = done_ref[pl.ds(slot_ref[at + u + PACK], 1), :]
            taken.append(jnp.where(low_row, low, high))
        for u in range(UN):
            source[pl.ds(at + u, 1), :] = taken[u]
        return 0

    lax.fori_loop(0, PACK // UN, fetch, 0)
    out_ref[...] = source[...].astype(BF)


def fetch_back(slots, done):
    return pl.pallas_call(
        fetch_kernel,
        in_specs=[
            pl.BlockSpec(memory_space=pltpu.SMEM),
            pl.BlockSpec(memory_space=pltpu.VMEM),
        ],
        out_specs=pl.BlockSpec(memory_space=pltpu.VMEM),
        out_shape=jax.ShapeDtypeStruct((PACK, 128), BF),
        scratch_shapes=[pltpu.VMEM((PACK, 128), F32)],
        compiler_params=pltpu.CompilerParams(vmem_limit_bytes=VMEM),
        name="fetch_back",
    )(slots, done)


def beside(sides, axis):
    forward = [(i, i + 1) for i in range(lax.axis_size(axis) - 1)]
    backward = [(target, source) for source, target in forward]
    return [
        lax.ppermute(sides[:, 1], axis, forward),
        lax.ppermute(sides[:, 0], axis, backward),
    ]


def ranks_of(owners):
    lanes = 128
    count = owners.shape[0]
    matches = (owners[None, :] == jnp.arange(DEV, dtype=jnp.int32)[:, None]).astype(BF)
    grouped = matches.reshape(DEV, count // lanes, lanes)
    index_row = jnp.arange(lanes, dtype=jnp.int32)
    strict = (index_row[:, None] < index_row[None, :]).astype(BF)
    within = jnp.einsum("dbi,ij->dbj", grouped, strict, preferred_element_type=F32)
    totals = jnp.sum(grouped.astype(F32), axis=2)
    before = jnp.cumsum(totals, axis=1) - totals
    ranking = jnp.sum(grouped.astype(F32) * (within + before[:, :, None]), axis=0)
    return ranking.reshape(count).astype(jnp.int32), matches, jnp.max(jnp.sum(totals, axis=1))


def place_of(owners, ranking, half, stride):
    return (ranking // half) * (DEV * stride) + owners * stride + ranking % half


def listed(matches, ranking, capacity, pieces):
    ranks = (ranking[:, None] == jnp.arange(capacity, dtype=jnp.int32)[None, :]).astype(BF)
    columns = jnp.concatenate([ranks * piece.astype(BF)[:, None] for piece in pieces], axis=1)
    return jnp.dot(matches, columns, preferred_element_type=F32).reshape(DEV, -1, capacity)


def code_rows(lists):
    _, count, capacity = lists.shape
    padded = jnp.pad(lists, ((0, 0), (0, EXTRA - count), (0, 128 - capacity)))
    return padded.reshape(DEV * EXTRA, 128)


def read_codes(packed, half, capacity, count):
    rows = packed.reshape(DEV, half + EXTRA, 128)
    return rows[:, half : half + count, :capacity].astype(jnp.int32)


def slot_pieces(slots):
    return [(slots + 1) // 64, (slots + 1) % 64]


def as_slots(high, low):
    coded = high * 64 + low
    return jnp.where(coded == 0, PTS, coded - 1)


def swap(values):
    return lax.all_to_all(values, ("gx", "gy"), split_axis=0, concat_axis=0, tiled=True)


def exchange(packed):
    rows = packed.shape[0]
    return swap(packed.reshape(DEV, rows // DEV, 128)).reshape(rows, 128)


def through_home(z_slots, z_dest, z_ranking, h_dest, done, weights):
    ranking, matches, _ = ranks_of(h_dest[0])
    h_lists = listed(matches, ranking, CAP, slot_pieces(h_dest[1]))
    h_lists = swap(h_lists.astype(jnp.int32).reshape(DEV, 2 * CAP))
    h_slots = as_slots(h_lists[:, :CAP], h_lists[:, CAP:]).reshape(-1)
    back_slots = z_slots.reshape(DEV, 2, HALF).transpose(1, 0, 2).reshape(-1)
    returned = exchange(fetch_back(back_slots, done))
    z_place = place_of(z_dest[0], z_ranking, HALF, HALF)
    h_place = place_of(h_dest[0], ranking, HALF, HALF)
    resent = relay(z_place, h_place, returned)
    return last_block(HALF, h_slots, exchange(resent), weights)


def local(
    feats,
    face_rows,
    neighbours,
    z_dest,
    h_dest,
    conv_weight,
    qkv_weight,
    out_weight,
    up_weight,
    down_weight,
    norm_gains,
):
    picked = jnp.take(feats, face_rows[0], axis=1)
    faces = beside(picked[:, 0:2], "gx") + beside(picked[:, 2:4], "gy")

    z_ranking, matches, _ = ranks_of(z_dest[0])
    z_place = place_of(z_dest[0], z_ranking, HALF, OUT_STRIDE)
    pieces = slot_pieces(z_dest[1]) + [h_dest[0], h_dest[1] // 64, h_dest[1] % 64]
    codes = code_rows(listed(matches, z_ranking, CAP, pieces))
    received = exchange(
        conv_send(neighbours, z_place, codes, feats, faces, conv_weight, norm_gains)
    )

    codes = read_codes(received, HALF, CAP, 5)
    z_slots = as_slots(codes[:, 0], codes[:, 1]).reshape(-1)
    owners = jnp.where(z_slots == PTS, DEV, codes[:, 2].reshape(-1))
    ranking, matches, most = ranks_of(owners)
    kept = jnp.logical_and(owners < DEV, ranking < ON_CAP)
    onward = jnp.where(kept, place_of(owners, ranking, ON_HALF, ON_STRIDE), 2 * ON_PACK)
    next_slots = (codes[:, 3] * 64 + codes[:, 4]).reshape(-1)
    lists = listed(matches, ranking, ON_CAP, slot_pieces(next_slots))
    most = most.astype(jnp.int32)
    fullest = jnp.stack([most // 64, most % 64]).astype(F32)
    fullest = jnp.broadcast_to(fullest[None, :, None], (DEV, 2, ON_CAP))
    codes = code_rows(jnp.concatenate([lists, fullest], axis=1))

    weights = (qkv_weight, out_weight, up_weight, down_weight, norm_gains.T)
    direct, done = first_block(z_slots, onward, received, codes, weights)
    direct = exchange(direct)
    codes = read_codes(direct, ON_HALF, ON_CAP, 4)
    direct_slots = as_slots(codes[:, 0], codes[:, 1]).reshape(-1)
    fits = jnp.max(codes[:, 2, 0] * 64 + codes[:, 3, 0]) <= ON_CAP
    return lax.cond(
        fits,
        lambda: last_block(ON_HALF, direct_slots, direct, weights),
        lambda: through_home(z_slots, z_dest, z_ranking, h_dest, done, weights),
    )


def solution(mesh):
    placed = (
        P(None, ("gx", "gy")),
        P(("gx", "gy"), None, None),
        P(None, ("gx", "gy")),
        P(None, ("gx", "gy")),
        P(None, ("gx", "gy")),
        P(),
        P(),
        P(),
        P(),
        P(),
        P(),
    )
    return jax.shard_map(
        local, mesh=mesh, in_specs=placed, out_specs=P(None, ("gx", "gy")), check_vma=False
    )
```

profile of v0, /device:TPU:1, one launch (start us, length us, event | category | flops | bytes accessed | tf_op | source)
XLA Modules:
  0.0 261.9 jit_solution(13179626734757889096)
XLA Ops:
  1.4 1.5 copy.81
  2.9 1.3 gather_fusion
  4.4 4.5 %collective-permute-start = (bf16[64,128]{1,0:T(8,128)(2,1)S(1)}, bf16[64,128]{1,0:T(8,128)(2,1)S(1)}, u32[]{:S(2)}, u32[]{:S(2)}) collective-permute-start(bf16[64,128]{1,0:T(8,128)(2,1)S(1)} %get-tuple-element.206), channel_id=1, source_target_pairs={{0,16},{16,32},{32,48},{48,64},{64,80},{80,96},{96,112},{1,17},{17... | collective-permute-start | bytes 49160 | tf_op jit(solution)/shard_map/ppermute | solution.py:439
  8.9 1.9 collective-permute-start.1
  10.9 3.2 %collective-permute-start.2 = (bf16[64,128]{1,0:T(8,128)(2,1)S(1)}, bf16[64,128]{1,0:T(8,128)(2,1)S(1)}, u32[]{:S(2)}, u32[]{:S(2)}) collective-permute-start(bf16[64,128]{1,0:T(8,128)(2,1)S(1)} %get-tuple-element.204), channel_id=1, source_target_pairs={{0,1},{1,2},{2,3},{3,4},{4,5},{5,6},{6,7},{7,8},{8,9},{9,10},{10,1... | collective-permute-start | bytes 49160 | tf_op jit(solution)/shard_map/ppermute | solution.py:439
  14.1 1.3 collective-permute-start.3
  15.9 0.8 fusion.32
  18.8 0.8 pad_bitcast_fusion.1.code_ref
  20.9 76.1 %conv_send.1 = bf16[4096,128]{1,0:T(8,128)(2,1)} custom-call(s32[27,4096]{1,0:T(8,128)} %near_ref.1, s32[4096]{0:T(1024)} %fusion.75.place_ref, f32[1024,128]{1,0:T(8,128)} %pad_bitcast_fusion.1.code_ref, bf16[64,4096]{1,0:T(8,128)(2,1)} %feats_ref.1, bf16[64,128]{1,0:T(8,128)(2,1)} %copy-done.15, bf16[64,128]{1,0:T(8,128)(2,1)} %copy-done.16, ...), custom_call_target="tpu_custom_call" | custom-call | flops 99999997952 | bytes 1000000 | tf_op jit(solution)/shard_map/conv_send/pallas_call | solution.py:197
  97.0 12.0 %all-to-all-start.3 = ((bf16[128,32,128]{2,1,0:T(8,128)(2,1)}), bf16[128,32,128]{2,1,0:T(8,128)(2,1)S(1)}, u32[]{:S(2)}, u32[]{:S(2)}) async-start(bf16[128,32,128]{2,1,0:T(8,128)(2,1)} %bitcast.75), calls=%async_computation.3 | async-start | bytes 2097152 | tf_op jit(solution)/shard_map/all_to_all | solution.py:489
  109.9 18.0 %all-to-all-done.3 = bf16[128,32,128]{2,1,0:T(8,128)(2,1)S(1)} async-done(((bf16[128,32,128]{2,1,0:T(8,128)(2,1)}), bf16[128,32,128]{2,1,0:T(8,128)(2,1)S(1)}, u32[]{:S(2)}, u32[]{:S(2)}) %all-to-all-start.3) | async-done | bytes 1048608 | tf_op jit(solution)/shard_map/all_to_all | solution.py:489
  128.5 1.6 fusion.57
  130.2 1.0 convert_reduce_fusion.1
  132.7 1.2 fusion.28
  136.2 0.8 pad_bitcast_fusion.code_ref
  137.0 51.6 %first_block.1 = (bf16[5120,128]{1,0:T(8,128)(2,1)}, f32[4104,128]{1,0:T(8,128)S(1)}) custom-call(s32[6144]{0:T(1024)} %copy-done.8, s32[6144]{0:T(1024)} %get-tuple-element.193.onward_ref, bf16[4096,128]{1,0:T(8,128)(2,1)} %bitcast.73, f32[1024,128]{1,0:T(8,128)} %pad_bitcast_fusion.code_ref, bf16[2,64,192]{2,1,0:T(8,128)(2,1)S(1)} %copy-done.12, ...), custom_call_target="tpu_custom_call" | custom-call | flops 40000000000 | bytes 1000000 | tf_op jit(solution)/shard_map/first_block/pallas_call | solution.py:366
  188.7 5.9 %all-to-all-start.4 = ((bf16[128,40,128]{2,1,0:T(8,128)(2,1)}), bf16[128,40,128]{2,1,0:T(8,128)(2,1)}, u32[]{:S(2)}, u32[]{:S(2)}) async-start(bf16[128,40,128]{2,1,0:T(8,128)(2,1)} %bitcast.74), calls=%async_computation.4 | async-start | bytes 2621440 | tf_op jit(solution)/shard_map/all_to_all | solution.py:489
  194.5 21.2 %all-to-all-done.4 = bf16[128,40,128]{2,1,0:T(8,128)(2,1)} async-done(((bf16[128,40,128]{2,1,0:T(8,128)(2,1)}), bf16[128,40,128]{2,1,0:T(8,128)(2,1)}, u32[]{:S(2)}, u32[]{:S(2)}) %all-to-all-start.4) | async-done | bytes 1310752 | tf_op jit(solution)/shard_map/all_to_all | solution.py:489
  215.8 1.0 slice_convert_fusion.1
  216.8 0.8 fusion.61
  218.3 42.8 %conditional.1 = (bf16[64,4096]{1,0:T(8,128)(2,1)S(1)}) conditional(s32[]{:T(128)} %convert_element_type.170, (s32[2,4096]{1,0:T(2,128)S(1)}, s32[4096]{0:T(1024)S(1)}, s32[2,4096]{1,0:T(2,128)S(1)}, s32[128,1,48]{2,1,0:T(1,128)S(1)}, f32[4104,128]{1,0:T(8,128)S(1)}, /*index=5*/bf16[2,64,192]{2,1,0:T(8,128)(2,1)S(1)}, ...), branch_computations={%region_9.13_spmd, %region_13.14_spmd} | conditional | flops 41243746304 | bytes 15787300 | solution.py:553
  219.2 0.8 copy.90.down_ref
  220.0 41.1 %last_block.3 = bf16[64,4096]{1,0:T(8,128)(2,1)S(1)} custom-call(s32[8192]{0:T(1024)} %select_n.150.slot_ref, bf16[5120,128]{1,0:T(8,128)(2,1)} %bitcast.14.in_ref, bf16[2,64,192]{2,1,0:T(8,128)(2,1)S(1)} %get-tuple-element.74.qkv_ref, bf16[2,64,64]{2,1,0:T(8,128)(2,1)S(1)} %get-tuple-element.75.outw_ref, bf16[2,64,256]{2,1,0:T(8,128)(2,1)S(1)} %get-tuple-element.76.up_ref, ...), custom_call_target="tpu_custom_call" | custom-call | flops 40000000000 | bytes 1000000 | tf_op jit(solution)/shard_map/cond/branch_1_fun/last_block/pallas_call | solution.py:366
  261.1 0.8 copy-done.19
  (85 shorter events, 10.6 us)
Async XLA Ops:
  0.0 15.4 %copy-start.6 = (s32[2,4096]{1,0:T(2,128)S(1)}, s32[2,4096]{1,0:T(2,128)}, u32[]{:S(2)}) copy-start(s32[2,4096]{1,0:T(2,128)} %param.17) | copy-start | bytes 98308
  0.0 15.5 %copy-start.9 = (s32[2,4096]{1,0:T(2,128)S(1)}, s32[2,4096]{1,0:T(2,128)}, u32[]{:S(2)}) copy-start(s32[2,4096]{1,0:T(2,128)} %param.16) | copy-start | bytes 98308
  4.4 15.3 %collective-permute-start = (bf16[64,128]{1,0:T(8,128)(2,1)S(1)}, bf16[64,128]{1,0:T(8,128)(2,1)S(1)}, u32[]{:S(2)}, u32[]{:S(2)}) collective-permute-start(bf16[64,128]{1,0:T(8,128)(2,1)S(1)} %get-tuple-element.206), channel_id=1, source_target_pairs={{0,16},{16,32},{32,48},{48,64},{64,80},{80,96},{96,112},{1,17},{17... | collective-permute-start | bytes 49160 | tf_op jit(solution)/shard_map/ppermute | solution.py:439
  8.9 10.8 %collective-permute-start.1 = (bf16[64,128]{1,0:T(8,128)(2,1)S(1)}, bf16[64,128]{1,0:T(8,128)(2,1)S(1)}, u32[]{:S(2)}, u32[]{:S(2)}) collective-permute-start(bf16[64,128]{1,0:T(8,128)(2,1)S(1)} %get-tuple-element.205), channel_id=1, source_target_pairs={{16,0},{32,16},{48,32},{64,48},{80,64},{96,80},{112,96},{17,1},{33... | collective-permute-start | bytes 49160 | tf_op jit(solution)/shard_map/ppermute | solution.py:440
  10.9 8.8 %collective-permute-start.2 = (bf16[64,128]{1,0:T(8,128)(2,1)S(1)}, bf16[64,128]{1,0:T(8,128)(2,1)S(1)}, u32[]{:S(2)}, u32[]{:S(2)}) collective-permute-start(bf16[64,128]{1,0:T(8,128)(2,1)S(1)} %get-tuple-element.204), channel_id=1, source_target_pairs={{0,1},{1,2},{2,3},{3,4},{4,5},{5,6},{6,7},{7,8},{8,9},{9,10},{10,1... | collective-permute-start | bytes 49160 | tf_op jit(solution)/shard_map/ppermute | solution.py:439
  14.1 5.7 %collective-permute-start.3 = (bf16[64,128]{1,0:T(8,128)(2,1)S(1)}, bf16[64,128]{1,0:T(8,128)(2,1)S(1)}, u32[]{:S(2)}, u32[]{:S(2)}) collective-permute-start(bf16[64,128]{1,0:T(8,128)(2,1)S(1)} %get-tuple-element.203), channel_id=1, source_target_pairs={{1,0},{2,1},{3,2},{4,3},{5,4},{6,5},{7,6},{8,7},{9,8},{10,9},{11,1... | collective-permute-start | bytes 49160 | tf_op jit(solution)/shard_map/ppermute | solution.py:440
  16.8 1.0 copy-start.1
  19.7 0.6 copy-start.15
  19.7 0.6 copy-start.16
  19.7 0.6 copy-start.17
  20.3 0.6 copy-start.18
  97.0 12.0 %copy-start.11 = (f32[5,64]{1,0:T(8,128)S(1)}, f32[5,64]{1,0:T(8,128)}, u32[]{:S(2)}) copy-start(f32[5,64]{1,0:T(8,128)} %gain_ref.1) | copy-start | bytes 3844
  97.0 12.1 %copy-start.5 = (bf16[2,256,64]{1,2,0:T(8,128)(2,1)S(1)}, bf16[2,256,64]{1,2,0:T(8,128)(2,1)}, u32[]{:S(2)}) copy-start(bf16[2,256,64]{1,2,0:T(8,128)(2,1)} %param.22) | copy-start | bytes 196612
  97.0 30.8 %all-to-all-start.3 = ((bf16[128,32,128]{2,1,0:T(8,128)(2,1)}), bf16[128,32,128]{2,1,0:T(8,128)(2,1)S(1)}, u32[]{:S(2)}, u32[]{:S(2)}) async-start(bf16[128,32,128]{2,1,0:T(8,128)(2,1)} %bitcast.75), calls=%async_computation.3 | async-start | bytes 2097152 | tf_op jit(solution)/shard_map/all_to_all | solution.py:489
  127.9 6.1 %copy-start = (bf16[128,32,128]{2,1,0:T(8,128)(2,1)}, bf16[128,32,128]{2,1,0:T(8,128)(2,1)S(1)}, u32[]{:S(2)}) copy-start(bf16[128,32,128]{2,1,0:T(8,128)(2,1)S(1)} %all-to-all-done.3) | copy-start | bytes 3145732
  134.2 1.8 copy-start.8
  135.2 1.9 copy-start.12
  135.2 1.8 copy-start.13
  135.2 1.8 copy-start.14
  188.7 29.6 %copy-start.2 = (s32[4096]{0:T(1024)S(1)}, s32[4096]{0:T(1024)}, u32[]{:S(2)}) copy-start(s32[4096]{0:T(1024)} %copy-done.1) | copy-start | bytes 49156
  188.7 29.6 %copy-start.7 = (s32[2,4096]{1,0:T(2,128)S(1)}, s32[2,4096]{1,0:T(2,128)}, u32[]{:S(2)}) copy-start(s32[2,4096]{1,0:T(2,128)} %param.17) | copy-start | bytes 98308
  188.7 29.6 %copy-start.10 = (s32[2,4096]{1,0:T(2,128)S(1)}, s32[2,4096]{1,0:T(2,128)}, u32[]{:S(2)}) copy-start(s32[2,4096]{1,0:T(2,128)} %param.16) | copy-start | bytes 98308
  188.7 27.1 %all-to-all-start.4 = ((bf16[128,40,128]{2,1,0:T(8,128)(2,1)}), bf16[128,40,128]{2,1,0:T(8,128)(2,1)}, u32[]{:S(2)}, u32[]{:S(2)}) async-start(bf16[128,40,128]{2,1,0:T(8,128)(2,1)} %bitcast.74), calls=%async_computation.4 | async-start | bytes 2621440 | tf_op jit(solution)/shard_map/all_to_all | solution.py:489
  261.1 0.8 copy-start.19
where the time goes:
time: 263 us; the launch traced here: 262 us
  Pallas kernels  169 us (64%)
  waiting for transfers between devices  39.2 us (15%)
  starting transfers between devices  28.8 us (11%)
  local copies, waits for them, and re-layouts  10.4 us (4%)
  other arithmetic  9.15 us (3%)
  matrix products  3.48 us (1%)
    pallas_call x2, Pallas kernels, block_call(): pl.pallas_call(kernel, in_specs=[pl.BlockSpec(memory_space=pltpu.SMEM)] *...  92.8 us
    pallas_call x1, Pallas kernels, conv_send(): pl.pallas_call(conv_kernel, in_specs=[pl.BlockSpec(memory_space=pltpu.VME...  76.1 us
    all_to_all x2, waiting for transfers between devices, swap(): lax.all_to_all(values, ('gx', 'gy'), split_axis=0, concat_axis=0, tiled=T...  39.2 us
    all_to_all x2, starting transfers between devices, swap(): lax.all_to_all(values, ('gx', 'gy'), split_axis=0, concat_axis=0, tiled=T...  17.9 us
    ppermute x2, starting transfers between devices, beside(): lax.ppermute(sides[:, 1], axis, forward)  7.71 us
  transfers between devices with their start and end apart: 6, of which 2 were waited for; matrix products, arithmetic and copies ran while one was open for 2% of the time, Pallas kernels for 0%

commit v1 on v0

--- a/solution.py
+++ b/solution.py
@@ -28,7 +28,7 @@
 ON_PACK = DEV * ON_STRIDE
 PAIRS = 13
 BLK = 512
-UN = 16
+UN = 64
 GROUP = 32
 GROUPS = PTS // GROUP
 LISTS = 4
@@ -308,7 +308,7 @@
     return residual + turned_dot(down_ref[j], hidden)
 
 
-def place_rows(half, slot_ref, in_ref, source, rows):
+def place_rows(half, span, slot_ref, in_ref, source, rows):
     unpack_rows(in_ref, source)
     count = in_ref.shape[0]
     stride = count // DEV
@@ -317,7 +317,7 @@
         for side in range(2):
             at = side * count + d * stride
             taken = [source[pl.ds(at + k, 1), :] for k in range(half)]
-            entry = d * 2 * half + side * half
+            entry = d * span + side * half
             for k in range(half):
                 rows[pl.ds(slot_ref[entry + k], 1), :] = taken[k]
         return 0
@@ -329,7 +329,7 @@
     slot_ref, onward_ref, in_ref, code_ref, qkv_ref, outw_ref, up_ref, down_ref, gain_ref,
     out_ref, done_ref, source, rows, mixed, values_ref,
 ):
-    place_rows(HALF, slot_ref, in_ref, source, rows)
+    place_rows(HALF, 128, slot_ref, in_ref, source, rows)
     done_ref[PTS:, :] = jnp.zeros((8, 128), F32)
 
     def patch(p, _):
@@ -341,7 +341,16 @@
         return 0
 
     lax.fori_loop(0, PTS // PATCH, patch, 0)
-    move_rows(DEV * CAP, lambda i: done_ref[pl.ds(slot_ref[i], 1), :], onward_ref, source)
+
+    def send(d, _):
+        for side in range(2):
+            entry = d * 128 + side * HALF
+            taken = [done_ref[pl.ds(slot_ref[entry + k], 1), :] for k in range(HALF)]
+            for k in range(HALF):
+                source[pl.ds(onward_ref[entry + k], 1), :] = taken[k]
+        return 0
+
+    lax.fori_loop(0, DEV, send, 0)
     put_codes(code_ref, source, ON_HALF)
     pack_rows(source, out_ref)
 
@@ -350,7 +359,7 @@
     half, slot_ref, in_ref, qkv_ref, outw_ref, up_ref, down_ref, gain_ref,
     out_ref, source, rows, mixed, values_ref,
 ):
-    place_rows(half, slot_ref, in_ref, source, rows)
+    place_rows(half, 2 * half, slot_ref, in_ref, source, rows)
 
     def patch(p, _):
         at = pl.multiple_of(p * PATCH, PATCH)
@@ -399,6 +408,84 @@
     )
 
 
+def plan_kernel(in_ref, slot_ref, onward_ref, code_ref, mine, turned, marks, picks):
+    def take(d, _):
+        tile = in_ref[pl.ds(pl.multiple_of(d * OUT_STRIDE + HALF - EXTRA, 16), 16), :]
+        mine[pl.ds(pl.multiple_of(d * EXTRA, EXTRA), EXTRA), :] = tile.astype(F32)[EXTRA:]
+        return 0
+
+    lax.fori_loop(0, DEV, take, 0, unroll=8)
+    high, low, owner, next_high, next_low = (
+        mine[pl.ds(p, DEV, stride=EXTRA), :] for p in range(5)
+    )
+    coded = (high * 64.0 + low).astype(jnp.int32)
+    slot_ref[...] = jnp.where(coded == 0, PTS, coded - 1)
+    owners = jnp.where(coded == 0, float(DEV), owner)
+    following = (next_high * 64.0 + next_low).astype(jnp.int32) + 1
+    turned[0] = owners.T
+    turned[1] = jnp.zeros((DEV, 128), F32)
+    turned[2] = (following >> 6).astype(F32).T
+    turned[3] = (following & 63).astype(F32).T
+    row = lax.broadcasted_iota(jnp.int32, (DEV, 128), 0)
+    row_f = row.astype(F32)
+    ahead = (row < lax.broadcasted_iota(jnp.int32, (DEV, 128), 1)).astype(F32).astype(BF)
+
+    def matches(r):
+        return (row_f == turned[0, pl.ds(r, 1), :]).astype(F32)
+
+    counts = lax.fori_loop(
+        0, CAP, lambda r, total: total + matches(r), jnp.zeros((DEV, 128), F32), unroll=8
+    )
+    most = jnp.max(jnp.sum(counts, axis=1, keepdims=True), axis=0, keepdims=True)
+    before = jnp.dot(counts.astype(BF), ahead, preferred_element_type=F32)
+    half_f = (row & (ON_CAP - 1)).astype(F32)
+    upper = row < ON_CAP
+
+    def rank(r, before):
+        match = matches(r)
+        ranking = jnp.sum(match * before, axis=0, keepdims=True)
+        turned[1, pl.ds(r, 1), :] = ranking
+        at = pl.ds(pl.multiple_of(r * 128, 128), 128)
+        marks[:, at] = match.astype(BF)
+        piece = jnp.where(upper, turned[2, pl.ds(r, 1), :], turned[3, pl.ds(r, 1), :])
+        picks[:, at] = jnp.where(half_f == ranking, piece, 0.0).astype(BF)
+        return before + match
+
+    lax.fori_loop(0, CAP, rank, before, unroll=4)
+    ranking = turned[1].T.astype(jnp.int32)
+    second = (ranking >= ON_HALF).astype(jnp.int32)
+    place = second * (ON_PACK - ON_HALF) + owners.astype(jnp.int32) * ON_STRIDE + ranking
+    kept = jnp.logical_and(coded > 0, ranking < ON_CAP)
+    onward_ref[...] = jnp.where(kept, place, 2 * ON_PACK)
+    lists = lax.dot_general(
+        picks[...], marks[...], (((1,), (1,)), ((), ())), preferred_element_type=F32
+    ).T
+    code_ref[...] = jnp.zeros((DEV, EXTRA, 128), F32)
+    code_ref[:, 0, :] = lists
+    code_ref[:, 1, :] = pltpu.roll(lists, ON_CAP, 1)
+    most = most.astype(jnp.int32)
+    code_ref[:, 2, :] = jnp.broadcast_to((most >> 6).astype(F32), (DEV, 128))
+    code_ref[:, 3, :] = jnp.broadcast_to((most & 63).astype(F32), (DEV, 128))
+
+
+def plan(received):
+    square = jax.ShapeDtypeStruct((DEV, 128), jnp.int32)
+    return pl.pallas_call(
+        plan_kernel,
+        in_specs=[pl.BlockSpec(memory_space=pltpu.VMEM)],
+        out_specs=[pl.BlockSpec(memory_space=pltpu.VMEM)] * 3,
+        out_shape=[square, square, jax.ShapeDtypeStruct((DEV, EXTRA, 128), F32)],
+        scratch_shapes=[
+            pltpu.VMEM((DEV * EXTRA, 128), F32),
+            pltpu.VMEM((4, DEV, 128), F32),
+            pltpu.VMEM((DEV, CAP * 128), BF),
+            pltpu.VMEM((DEV, CAP * 128), BF),
+        ],
+        compiler_params=pltpu.CompilerParams(vmem_limit_bytes=VMEM),
+        name="plan",
+    )(received)
+
+
 def fetch_kernel(slot_ref, done_ref, out_ref, source):
     low_row = low_lanes(1)
 
@@ -531,21 +618,11 @@
         conv_send(neighbours, z_place, codes, feats, faces, conv_weight, norm_gains)
     )
 
-    codes = read_codes(received, HALF, CAP, 5)
-    z_slots = as_slots(codes[:, 0], codes[:, 1]).reshape(-1)
-    owners = jnp.where(z_slots == PTS, DEV, codes[:, 2].reshape(-1))
-    ranking, matches, most = ranks_of(owners)
-    kept = jnp.logical_and(owners < DEV, ranking < ON_CAP)
-    onward = jnp.where(kept, place_of(owners, ranking, ON_HALF, ON_STRIDE), 2 * ON_PACK)
-    next_slots = (codes[:, 3] * 64 + codes[:, 4]).reshape(-1)
-    lists = listed(matches, ranking, ON_CAP, slot_pieces(next_slots))
-    most = most.astype(jnp.int32)
-    fullest = jnp.stack([most // 64, most % 64]).astype(F32)
-    fullest = jnp.broadcast_to(fullest[None, :, None], (DEV, 2, ON_CAP))
-    codes = code_rows(jnp.concatenate([lists, fullest], axis=1))
-
+    slots, onward, codes = plan(received)
+    z_slots = slots[:, :CAP]
+    codes = codes.reshape(DEV * EXTRA, 128)
     weights = (qkv_weight, out_weight, up_weight, down_weight, norm_gains.T)
-    direct, done = first_block(z_slots, onward, received, codes, weights)
+    direct, done = first_block(slots.reshape(-1), onward.reshape(-1), received, codes, weights)
     direct = exchange(direct)
     codes = read_codes(direct, ON_HALF, ON_CAP, 4)
     direct_slots = as_slots(codes[:, 0], codes[:, 1]).reshape(-1)

time: 263 us -> 259 us (0.985)
  other arithmetic: 9.15 us -> 4.77 us
  Pallas kernels: 169 us -> 173 us
    pallas_call x0 -> x1, Pallas kernels: none -> 4.92 us  [plan(): pl.pallas_call(plan_kernel, in_specs=[pl.BlockSpec(memory_space=pltpu.VME...]
    unnamed x39 -> x37, local copies, waits for them, and re-layouts: 4.41 us -> 5.37 us
where the time goes in v1:
time: 259 us; the launch traced here: 258 us
  Pallas kernels  173 us (67%)
  waiting for transfers between devices  39.2 us (15%)
  starting transfers between devices  28.8 us (11%)
  local copies, waits for them, and re-layouts  9.38 us (4%)
  other arithmetic  4.77 us (2%)
    pallas_call x2, Pallas kernels, block_call(): pl.pallas_call(kernel, in_specs=[pl.BlockSpec(memory_space=pltpu.SMEM)] *...  93.2 us
    pallas_call x1, Pallas kernels, conv_send(): pl.pallas_call(conv_kernel, in_specs=[pl.BlockSpec(memory_space=pltpu.VME...  75.2 us
    all_to_all x2, waiting for transfers between devices, swap(): lax.all_to_all(values, ('gx', 'gy'), split_axis=0, concat_axis=0, tiled=T...  39.2 us
    all_to_all x2, starting transfers between devices, swap(): lax.all_to_all(values, ('gx', 'gy'), split_axis=0, concat_axis=0, tiled=T...  17.9 us
    ppermute x2, starting transfers between devices, beside(): lax.ppermute(sides[:, 1], axis, forward)  7.71 us
    unnamed x37, local copies, waits for them, and re-layouts  5.37 us
  transfers between devices with their start and end apart: 6, of which 2 were waited for; matrix products, arithmetic and copies ran while one was open for 2% of the time, Pallas kernels for 0%

profile of v1, /device:TPU:1, one launch (start us, length us, event | category | flops | bytes accessed | tf_op | source)
XLA Modules:
  0.0 258.2 jit_solution(4839672585520221690)
XLA Ops:
  1.4 1.5 copy.59
  2.9 1.3 gather_fusion
  4.4 4.5 %collective-permute-start = (bf16[64,128]{1,0:T(8,128)(2,1)S(1)}, bf16[64,128]{1,0:T(8,128)(2,1)S(1)}, u32[]{:S(2)}, u32[]{:S(2)}) collective-permute-start(bf16[64,128]{1,0:T(8,128)(2,1)S(1)} %get-tuple-element.186), channel_id=1, source_target_pairs={{0,16},{16,32},{32,48},{48,64},{64,80},{80,96},{96,112},{1,17},{17... | collective-permute-start | bytes 49160 | tf_op jit(solution)/shard_map/ppermute | solution.py:526
  8.9 1.9 collective-permute-start.1
  10.9 3.2 %collective-permute-start.2 = (bf16[64,128]{1,0:T(8,128)(2,1)S(1)}, bf16[64,128]{1,0:T(8,128)(2,1)S(1)}, u32[]{:S(2)}, u32[]{:S(2)}) collective-permute-start(bf16[64,128]{1,0:T(8,128)(2,1)S(1)} %get-tuple-element.184), channel_id=1, source_target_pairs={{0,1},{1,2},{2,3},{3,4},{4,5},{5,6},{6,7},{7,8},{8,9},{9,10},{10,1... | collective-permute-start | bytes 49160 | tf_op jit(solution)/shard_map/ppermute | solution.py:526
  14.1 1.3 collective-permute-start.3
  15.9 0.8 fusion.28
  17.9 0.7 fusion.31
  18.8 0.8 pad_bitcast_fusion.code_ref
  20.9 75.2 %conv_send.1 = bf16[4096,128]{1,0:T(8,128)(2,1)} custom-call(s32[27,4096]{1,0:T(8,128)} %near_ref.1, s32[4096]{0:T(1024)} %fusion.49.place_ref, f32[1024,128]{1,0:T(8,128)} %pad_bitcast_fusion.code_ref, bf16[64,4096]{1,0:T(8,128)(2,1)} %feats_ref.1, bf16[64,128]{1,0:T(8,128)(2,1)} %copy-done.14, bf16[64,128]{1,0:T(8,128)(2,1)} %copy-done.15, ...), custom_call_target="tpu_custom_call" | custom-call | flops 99999997952 | bytes 1000000 | tf_op jit(solution)/shard_map/conv_send/pallas_call | solution.py:197
  96.1 12.0 %all-to-all-start.3 = ((bf16[128,32,128]{2,1,0:T(8,128)(2,1)}), bf16[128,32,128]{2,1,0:T(8,128)(2,1)S(1)}, u32[]{:S(2)}, u32[]{:S(2)}) async-start(bf16[128,32,128]{2,1,0:T(8,128)(2,1)} %bitcast.69), calls=%async_computation.3 | async-start | bytes 2097152 | tf_op jit(solution)/shard_map/all_to_all | solution.py:576
  108.3 0.8 copy.63.down_ref
  109.0 18.0 %all-to-all-done.3 = bf16[128,32,128]{2,1,0:T(8,128)(2,1)S(1)} async-done(((bf16[128,32,128]{2,1,0:T(8,128)(2,1)}), bf16[128,32,128]{2,1,0:T(8,128)(2,1)S(1)}, u32[]{:S(2)}, u32[]{:S(2)}) %all-to-all-start.3) | async-done | bytes 1048608 | tf_op jit(solution)/shard_map/all_to_all | solution.py:576
  127.0 1.0 copy-done
  127.9 4.9 %plan.1 = (s32[128,128]{1,0:T(8,128)S(1)}, s32[128,128]{1,0:T(8,128)}, f32[128,8,128]{2,1,0:T(8,128)}) custom-call(bf16[4096,128]{1,0:T(8,128)(2,1)} %bitcast.65), custom_call_target="tpu_custom_call" | custom-call | tf_op jit(solution)/shard_map/plan/pallas_call | solution.py:473
  132.9 52.0 %first_block.1 = (bf16[5120,128]{1,0:T(8,128)(2,1)}, f32[4104,128]{1,0:T(8,128)S(1)}) custom-call(s32[16384]{0:T(1024)S(1)} %bitcast.85, s32[16384]{0:T(1024)} %bitcast.94, bf16[4096,128]{1,0:T(8,128)(2,1)} %bitcast.66, f32[1024,128]{1,0:T(8,128)} %bitcast.93, bf16[2,64,192]{2,1,0:T(8,128)(2,1)S(1)} %copy-done.11, bf16[2,64,64]{2,1,0:T(8,128)(2,1)S(1)} %copy-done.13, ...), custom_call_target="tpu_custom_call" | custom-call | flops 40000000000 | bytes 1000000 | tf_op jit(solution)/shard_map/first_block/pallas_call | solution.py:375
  184.9 5.9 %all-to-all-start.4 = ((bf16[128,40,128]{2,1,0:T(8,128)(2,1)}), bf16[128,40,128]{2,1,0:T(8,128)(2,1)}, u32[]{:S(2)}, u32[]{:S(2)}) async-start(bf16[128,40,128]{2,1,0:T(8,128)(2,1)} %bitcast.68), calls=%async_computation.4 | async-start | bytes 2621440 | tf_op jit(solution)/shard_map/all_to_all | solution.py:576
  190.8 21.2 %all-to-all-done.4 = bf16[128,40,128]{2,1,0:T(8,128)(2,1)} async-done(((bf16[128,40,128]{2,1,0:T(8,128)(2,1)}), bf16[128,40,128]{2,1,0:T(8,128)(2,1)}, u32[]{:S(2)}, u32[]{:S(2)}) %all-to-all-start.4) | async-done | bytes 1310752 | tf_op jit(solution)/shard_map/all_to_all | solution.py:576
  212.0 1.0 slice_convert_fusion
  213.0 0.8 fusion.46
  214.5 42.9 %conditional.1 = (bf16[64,4096]{1,0:T(8,128)(2,1)S(1)}) conditional(s32[]{:T(128)} %convert_element_type.112, (s32[2,4096]{1,0:T(2,128)S(1)}, s32[4096]{0:T(1024)S(1)}, s32[2,4096]{1,0:T(2,128)S(1)}, s32[128,128]{1,0:T(8,128)S(1)}, f32[4104,128]{1,0:T(8,128)S(1)}, /*index=5*/bf16[2,64,192]{2,1,0:T(8,128)(2,1)S(1)}, bf16[2,64,64]{2,1,0:T(8,128)(2,1)S(1)}, ...), branch_computations={%region_4.8_spmd, %region_8.9_spmd} | conditional | flops 41243746304 | bytes 15918372 | solution.py:630
  215.5 0.8 copy.67.down_ref
  216.2 41.1 %last_block.3 = bf16[64,4096]{1,0:T(8,128)(2,1)S(1)} custom-call(s32[8192]{0:T(1024)} %select_n.94.slot_ref, bf16[5120,128]{1,0:T(8,128)(2,1)} %bitcast.14.in_ref, bf16[2,64,192]{2,1,0:T(8,128)(2,1)S(1)} %get-tuple-element.74.qkv_ref, bf16[2,64,64]{2,1,0:T(8,128)(2,1)S(1)} %get-tuple-element.75.outw_ref, bf16[2,64,256]{2,1,0:T(8,128)(2,1)S(1)} %get-tuple-element.76.up_ref, ...), custom_call_target="tpu_custom_call" | custom-call | flops 40000000000 | bytes 1000000 | tf_op jit(solution)/shard_map/cond/branch_1_fun/last_block/pallas_call | solution.py:375
  257.4 0.8 copy-done.18
  (62 shorter events, 5.4 us)
Async XLA Ops:
  0.0 15.4 %copy-start.6 = (s32[2,4096]{1,0:T(2,128)S(1)}, s32[2,4096]{1,0:T(2,128)}, u32[]{:S(2)}) copy-start(s32[2,4096]{1,0:T(2,128)} %param.17) | copy-start | bytes 98308
  0.0 15.5 %copy-start.8 = (s32[2,4096]{1,0:T(2,128)S(1)}, s32[2,4096]{1,0:T(2,128)}, u32[]{:S(2)}) copy-start(s32[2,4096]{1,0:T(2,128)} %param.16) | copy-start | bytes 98308
  4.4 15.3 %collective-permute-start = (bf16[64,128]{1,0:T(8,128)(2,1)S(1)}, bf16[64,128]{1,0:T(8,128)(2,1)S(1)}, u32[]{:S(2)}, u32[]{:S(2)}) collective-permute-start(bf16[64,128]{1,0:T(8,128)(2,1)S(1)} %get-tuple-element.186), channel_id=1, source_target_pairs={{0,16},{16,32},{32,48},{48,64},{64,80},{80,96},{96,112},{1,17},{17... | collective-permute-start | bytes 49160 | tf_op jit(solution)/shard_map/ppermute | solution.py:526
  8.9 10.8 %collective-permute-start.1 = (bf16[64,128]{1,0:T(8,128)(2,1)S(1)}, bf16[64,128]{1,0:T(8,128)(2,1)S(1)}, u32[]{:S(2)}, u32[]{:S(2)}) collective-permute-start(bf16[64,128]{1,0:T(8,128)(2,1)S(1)} %get-tuple-element.185), channel_id=1, source_target_pairs={{16,0},{32,16},{48,32},{64,48},{80,64},{96,80},{112,96},{17,1},{33... | collective-permute-start | bytes 49160 | tf_op jit(solution)/shard_map/ppermute | solution.py:527
  10.9 8.8 %collective-permute-start.2 = (bf16[64,128]{1,0:T(8,128)(2,1)S(1)}, bf16[64,128]{1,0:T(8,128)(2,1)S(1)}, u32[]{:S(2)}, u32[]{:S(2)}) collective-permute-start(bf16[64,128]{1,0:T(8,128)(2,1)S(1)} %get-tuple-element.184), channel_id=1, source_target_pairs={{0,1},{1,2},{2,3},{3,4},{4,5},{5,6},{6,7},{7,8},{8,9},{9,10},{10,1... | collective-permute-start | bytes 49160 | tf_op jit(solution)/shard_map/ppermute | solution.py:526
  14.1 5.7 %collective-permute-start.3 = (bf16[64,128]{1,0:T(8,128)(2,1)S(1)}, bf16[64,128]{1,0:T(8,128)(2,1)S(1)}, u32[]{:S(2)}, u32[]{:S(2)}) collective-permute-start(bf16[64,128]{1,0:T(8,128)(2,1)S(1)} %get-tuple-element.183), channel_id=1, source_target_pairs={{1,0},{2,1},{3,2},{4,3},{5,4},{6,5},{7,6},{8,7},{9,8},{10,9},{11,1... | collective-permute-start | bytes 49160 | tf_op jit(solution)/shard_map/ppermute | solution.py:527
  16.8 1.0 copy-start.1
  19.7 0.6 copy-start.14
  19.7 0.6 copy-start.15
  19.7 0.6 copy-start.16
  20.3 0.6 copy-start.17
  96.1 12.1 %copy-start.10 = (f32[5,64]{1,0:T(8,128)S(1)}, f32[5,64]{1,0:T(8,128)}, u32[]{:S(2)}) copy-start(f32[5,64]{1,0:T(8,128)} %gain_ref.1) | copy-start | bytes 3844
  96.1 12.2 %copy-start.5 = (bf16[2,256,64]{1,2,0:T(8,128)(2,1)S(1)}, bf16[2,256,64]{1,2,0:T(8,128)(2,1)}, u32[]{:S(2)}) copy-start(bf16[2,256,64]{1,2,0:T(8,128)(2,1)} %param.22) | copy-start | bytes 196612
  96.1 36.8 %copy-start.11 = (bf16[2,64,192]{2,1,0:T(8,128)(2,1)S(1)}, bf16[2,64,192]{2,1,0:T(8,128)(2,1)}, u32[]{:S(2)}) copy-start(bf16[2,64,192]{2,1,0:T(8,128)(2,1)} %qkv_ref.1) | copy-start | bytes 147460
  96.1 36.8 %copy-start.12 = (bf16[2,64,256]{2,1,0:T(8,128)(2,1)S(1)}, bf16[2,64,256]{2,1,0:T(8,128)(2,1)}, u32[]{:S(2)}) copy-start(bf16[2,64,256]{2,1,0:T(8,128)(2,1)} %up_ref.1) | copy-start | bytes 196612
  96.1 36.7 %copy-start.13 = (bf16[2,64,64]{2,1,0:T(8,128)(2,1)S(1)}, bf16[2,64,64]{2,1,0:T(8,128)(2,1)}, u32[]{:S(2)}) copy-start(bf16[2,64,64]{2,1,0:T(8,128)(2,1)} %outw_ref.1) | copy-start | bytes 49156
  96.1 30.8 %all-to-all-start.3 = ((bf16[128,32,128]{2,1,0:T(8,128)(2,1)}), bf16[128,32,128]{2,1,0:T(8,128)(2,1)S(1)}, u32[]{:S(2)}, u32[]{:S(2)}) async-start(bf16[128,32,128]{2,1,0:T(8,128)(2,1)} %bitcast.69), calls=%async_computation.3 | async-start | bytes 2097152 | tf_op jit(solution)/shard_map/all_to_all | solution.py:576
  127.0 1.0 copy-start
  184.9 29.6 %copy-start.2 = (s32[4096]{0:T(1024)S(1)}, s32[4096]{0:T(1024)}, u32[]{:S(2)}) copy-start(s32[4096]{0:T(1024)} %copy-done.1) | copy-start | bytes 49156
  184.9 29.6 %copy-start.7 = (s32[2,4096]{1,0:T(2,128)S(1)}, s32[2,4096]{1,0:T(2,128)}, u32[]{:S(2)}) copy-start(s32[2,4096]{1,0:T(2,128)} %param.17) | copy-start | bytes 98308
  184.9 29.6 %copy-start.9 = (s32[2,4096]{1,0:T(2,128)S(1)}, s32[2,4096]{1,0:T(2,128)}, u32[]{:S(2)}) copy-start(s32[2,4096]{1,0:T(2,128)} %param.16) | copy-start | bytes 98308
  184.9 27.1 %all-to-all-start.4 = ((bf16[128,40,128]{2,1,0:T(8,128)(2,1)}), bf16[128,40,128]{2,1,0:T(8,128)(2,1)}, u32[]{:S(2)}, u32[]{:S(2)}) async-start(bf16[128,40,128]{2,1,0:T(8,128)(2,1)} %bitcast.68), calls=%async_computation.4 | async-start | bytes 2621440 | tf_op jit(solution)/shard_map/all_to_all | solution.py:576
  257.4 0.8 copy-start.18

commit v2 on v1

--- a/solution.py
+++ b/solution.py
@@ -313,13 +313,22 @@
     count = in_ref.shape[0]
     stride = count // DEV
 
+    first = CAP // 3 if 2 * half == CAP else CAP
+
     def place(d, _):
-        for side in range(2):
-            at = side * count + d * stride
-            taken = [source[pl.ds(at + k, 1), :] for k in range(half)]
-            entry = d * span + side * half
-            for k in range(half):
-                rows[pl.ds(slot_ref[entry + k], 1), :] = taken[k]
+        def some(ranks):
+            taken = [
+                source[pl.ds(k // half * count + d * stride + k % half, 1), :] for k in ranks
+            ]
+            for k, value in zip(ranks, taken):
+                rows[pl.ds(slot_ref[d * span + k], 1), :] = value
+
+        some(range(first))
+
+        @pl.when(slot_ref[d * span + first] < PTS)
+        def _():
+            some(range(first, 2 * half))
+
         return 0
 
     lax.fori_loop(0, DEV, place, 0)
@@ -343,11 +352,17 @@
     lax.fori_loop(0, PTS // PATCH, patch, 0)
 
     def send(d, _):
-        for side in range(2):
-            entry = d * 128 + side * HALF
-            taken = [done_ref[pl.ds(slot_ref[entry + k], 1), :] for k in range(HALF)]
-            for k in range(HALF):
-                source[pl.ds(onward_ref[entry + k], 1), :] = taken[k]
+        def some(ranks):
+            taken = [done_ref[pl.ds(slot_ref[d * 128 + k], 1), :] for k in ranks]
+            for k, value in zip(ranks, taken):
+                source[pl.ds(onward_ref[d * 128 + k], 1), :] = value
+
+        some(range(CAP // 3))
+
+        @pl.when(slot_ref[d * 128 + CAP // 3] < PTS)
+        def _():
+            some(range(CAP // 3, CAP))
+
         return 0
 
     lax.fori_loop(0, DEV, send, 0)

time: 259 us -> 256 us (0.988)
  Pallas kernels: 173 us -> 170 us
    pallas_call x2, Pallas kernels: 93.2 us -> 89.8 us  [block_call(): pl.pallas_call(kernel, in_specs=[pl.BlockSpec(memory_space=pltpu.SMEM)] *...]
where the time goes in v2:
time: 256 us; the launch traced here: 255 us
  Pallas kernels  170 us (66%)
  waiting for transfers between devices  39.2 us (15%)
  starting transfers between devices  28.8 us (11%)
  local copies, waits for them, and re-layouts  9.38 us (4%)
  other arithmetic  4.77 us (2%)
    pallas_call x2, Pallas kernels, block_call(): pl.pallas_call(kernel, in_specs=[pl.BlockSpec(memory_space=pltpu.SMEM)] *...  89.8 us
    pallas_call x1, Pallas kernels, conv_send(): pl.pallas_call(conv_kernel, in_specs=[pl.BlockSpec(memory_space=pltpu.VME...  75.2 us
    all_to_all x2, waiting for transfers between devices, swap(): lax.all_to_all(values, ('gx', 'gy'), split_axis=0, concat_axis=0, tiled=T...  39.2 us
    all_to_all x2, starting transfers between devices, swap(): lax.all_to_all(values, ('gx', 'gy'), split_axis=0, concat_axis=0, tiled=T...  17.9 us
    ppermute x2, starting transfers between devices, beside(): lax.ppermute(sides[:, 1], axis, forward)  7.71 us
    unnamed x37, local copies, waits for them, and re-layouts  5.37 us
  transfers between devices with their start and end apart: 6, of which 2 were waited for; matrix products, arithmetic and copies ran while one was open for 2% of the time, Pallas kernels for 0%

profile of v2, /device:TPU:1, one launch (start us, length us, event | category | flops | bytes accessed | tf_op | source)
XLA Modules:
  0.0 254.8 jit_solution(16023013497855293007)
XLA Ops:
  1.4 1.5 copy.59
  2.9 1.3 gather_fusion
  4.4 4.5 %collective-permute-start = (bf16[64,128]{1,0:T(8,128)(2,1)S(1)}, bf16[64,128]{1,0:T(8,128)(2,1)S(1)}, u32[]{:S(2)}, u32[]{:S(2)}) collective-permute-start(bf16[64,128]{1,0:T(8,128)(2,1)S(1)} %get-tuple-element.186), channel_id=1, source_target_pairs={{0,16},{16,32},{32,48},{48,64},{64,80},{80,96},{96,112},{1,17},{17... | collective-permute-start | bytes 49160 | tf_op jit(solution)/shard_map/ppermute | solution.py:541
  8.9 1.9 collective-permute-start.1
  10.9 3.2 %collective-permute-start.2 = (bf16[64,128]{1,0:T(8,128)(2,1)S(1)}, bf16[64,128]{1,0:T(8,128)(2,1)S(1)}, u32[]{:S(2)}, u32[]{:S(2)}) collective-permute-start(bf16[64,128]{1,0:T(8,128)(2,1)S(1)} %get-tuple-element.184), channel_id=1, source_target_pairs={{0,1},{1,2},{2,3},{3,4},{4,5},{5,6},{6,7},{7,8},{8,9},{9,10},{10,1... | collective-permute-start | bytes 49160 | tf_op jit(solution)/shard_map/ppermute | solution.py:541
  14.1 1.3 collective-permute-start.3
  15.9 0.8 fusion.28
  17.9 0.7 fusion.31
  18.8 0.8 pad_bitcast_fusion.code_ref
  20.9 75.2 %conv_send.1 = bf16[4096,128]{1,0:T(8,128)(2,1)} custom-call(s32[27,4096]{1,0:T(8,128)} %near_ref.1, s32[4096]{0:T(1024)} %fusion.49.place_ref, f32[1024,128]{1,0:T(8,128)} %pad_bitcast_fusion.code_ref, bf16[64,4096]{1,0:T(8,128)(2,1)} %feats_ref.1, bf16[64,128]{1,0:T(8,128)(2,1)} %copy-done.14, bf16[64,128]{1,0:T(8,128)(2,1)} %copy-done.15, ...), custom_call_target="tpu_custom_call" | custom-call | flops 99999997952 | bytes 1000000 | tf_op jit(solution)/shard_map/conv_send/pallas_call | solution.py:197
  96.1 12.0 %all-to-all-start.3 = ((bf16[128,32,128]{2,1,0:T(8,128)(2,1)}), bf16[128,32,128]{2,1,0:T(8,128)(2,1)S(1)}, u32[]{:S(2)}, u32[]{:S(2)}) async-start(bf16[128,32,128]{2,1,0:T(8,128)(2,1)} %bitcast.69), calls=%async_computation.3 | async-start | bytes 2097152 | tf_op jit(solution)/shard_map/all_to_all | solution.py:591
  108.3 0.8 copy.63.down_ref
  109.0 18.0 %all-to-all-done.3 = bf16[128,32,128]{2,1,0:T(8,128)(2,1)S(1)} async-done(((bf16[128,32,128]{2,1,0:T(8,128)(2,1)}), bf16[128,32,128]{2,1,0:T(8,128)(2,1)S(1)}, u32[]{:S(2)}, u32[]{:S(2)}) %all-to-all-start.3) | async-done | bytes 1048608 | tf_op jit(solution)/shard_map/all_to_all | solution.py:591
  127.0 1.0 copy-done
  127.9 4.9 %plan.1 = (s32[128,128]{1,0:T(8,128)S(1)}, s32[128,128]{1,0:T(8,128)}, f32[128,8,128]{2,1,0:T(8,128)}) custom-call(bf16[4096,128]{1,0:T(8,128)(2,1)} %bitcast.65), custom_call_target="tpu_custom_call" | custom-call | tf_op jit(solution)/shard_map/plan/pallas_call | solution.py:488
  132.9 49.2 %first_block.1 = (bf16[5120,128]{1,0:T(8,128)(2,1)}, f32[4104,128]{1,0:T(8,128)S(1)}) custom-call(s32[16384]{0:T(1024)S(1)} %bitcast.85, s32[16384]{0:T(1024)} %bitcast.94, bf16[4096,128]{1,0:T(8,128)(2,1)} %bitcast.66, f32[1024,128]{1,0:T(8,128)} %bitcast.93, bf16[2,64,192]{2,1,0:T(8,128)(2,1)S(1)} %copy-done.11, bf16[2,64,64]{2,1,0:T(8,128)(2,1)S(1)} %copy-done.13, ...), custom_call_target="tpu_custom_call" | custom-call | flops 40000000000 | bytes 1000000 | tf_op jit(solution)/shard_map/first_block/pallas_call | solution.py:390
  182.1 5.9 %all-to-all-start.4 = ((bf16[128,40,128]{2,1,0:T(8,128)(2,1)}), bf16[128,40,128]{2,1,0:T(8,128)(2,1)}, u32[]{:S(2)}, u32[]{:S(2)}) async-start(bf16[128,40,128]{2,1,0:T(8,128)(2,1)} %bitcast.68), calls=%async_computation.4 | async-start | bytes 2621440 | tf_op jit(solution)/shard_map/all_to_all | solution.py:591
  188.0 21.2 %all-to-all-done.4 = bf16[128,40,128]{2,1,0:T(8,128)(2,1)} async-done(((bf16[128,40,128]{2,1,0:T(8,128)(2,1)}), bf16[128,40,128]{2,1,0:T(8,128)(2,1)}, u32[]{:S(2)}, u32[]{:S(2)}) %all-to-all-start.4) | async-done | bytes 1310752 | tf_op jit(solution)/shard_map/all_to_all | solution.py:591
  209.2 1.0 slice_convert_fusion
  210.2 0.8 fusion.46
  211.7 42.3 %conditional.1 = (bf16[64,4096]{1,0:T(8,128)(2,1)S(1)}) conditional(s32[]{:T(128)} %convert_element_type.112, (s32[2,4096]{1,0:T(2,128)S(1)}, s32[4096]{0:T(1024)S(1)}, s32[2,4096]{1,0:T(2,128)S(1)}, s32[128,128]{1,0:T(8,128)S(1)}, f32[4104,128]{1,0:T(8,128)S(1)}, /*index=5*/bf16[2,64,192]{2,1,0:T(8,128)(2,1)S(1)}, bf16[2,64,64]{2,1,0:T(8,128)(2,1)S(1)}, ...), branch_computations={%region_4.8_spmd, %region_8.9_spmd} | conditional | flops 41243746304 | bytes 15918372 | solution.py:645
  212.7 0.8 copy.67.down_ref
  213.4 40.6 %last_block.3 = bf16[64,4096]{1,0:T(8,128)(2,1)S(1)} custom-call(s32[8192]{0:T(1024)} %select_n.94.slot_ref, bf16[5120,128]{1,0:T(8,128)(2,1)} %bitcast.14.in_ref, bf16[2,64,192]{2,1,0:T(8,128)(2,1)S(1)} %get-tuple-element.74.qkv_ref, bf16[2,64,64]{2,1,0:T(8,128)(2,1)S(1)} %get-tuple-element.75.outw_ref, bf16[2,64,256]{2,1,0:T(8,128)(2,1)S(1)} %get-tuple-element.76.up_ref, ...), custom_call_target="tpu_custom_call" | custom-call | flops 40000000000 | bytes 1000000 | tf_op jit(solution)/shard_map/cond/branch_1_fun/last_block/pallas_call | solution.py:390
  254.0 0.8 copy-done.18
  (62 shorter events, 5.4 us)
Async XLA Ops:
  0.0 15.4 %copy-start.6 = (s32[2,4096]{1,0:T(2,128)S(1)}, s32[2,4096]{1,0:T(2,128)}, u32[]{:S(2)}) copy-start(s32[2,4096]{1,0:T(2,128)} %param.17) | copy-start | bytes 98308
  0.0 15.5 %copy-start.8 = (s32[2,4096]{1,0:T(2,128)S(1)}, s32[2,4096]{1,0:T(2,128)}, u32[]{:S(2)}) copy-start(s32[2,4096]{1,0:T(2,128)} %param.16) | copy-start | bytes 98308
  4.4 15.3 %collective-permute-start = (bf16[64,128]{1,0:T(8,128)(2,1)S(1)}, bf16[64,128]{1,0:T(8,128)(2,1)S(1)}, u32[]{:S(2)}, u32[]{:S(2)}) collective-permute-start(bf16[64,128]{1,0:T(8,128)(2,1)S(1)} %get-tuple-element.186), channel_id=1, source_target_pairs={{0,16},{16,32},{32,48},{48,64},{64,80},{80,96},{96,112},{1,17},{17... | collective-permute-start | bytes 49160 | tf_op jit(solution)/shard_map/ppermute | solution.py:541
  8.9 10.8 %collective-permute-start.1 = (bf16[64,128]{1,0:T(8,128)(2,1)S(1)}, bf16[64,128]{1,0:T(8,128)(2,1)S(1)}, u32[]{:S(2)}, u32[]{:S(2)}) collective-permute-start(bf16[64,128]{1,0:T(8,128)(2,1)S(1)} %get-tuple-element.185), channel_id=1, source_target_pairs={{16,0},{32,16},{48,32},{64,48},{80,64},{96,80},{112,96},{17,1},{33... | collective-permute-start | bytes 49160 | tf_op jit(solution)/shard_map/ppermute | solution.py:542
  10.9 8.9 %collective-permute-start.2 = (bf16[64,128]{1,0:T(8,128)(2,1)S(1)}, bf16[64,128]{1,0:T(8,128)(2,1)S(1)}, u32[]{:S(2)}, u32[]{:S(2)}) collective-permute-start(bf16[64,128]{1,0:T(8,128)(2,1)S(1)} %get-tuple-element.184), channel_id=1, source_target_pairs={{0,1},{1,2},{2,3},{3,4},{4,5},{5,6},{6,7},{7,8},{8,9},{9,10},{10,1... | collective-permute-start | bytes 49160 | tf_op jit(solution)/shard_map/ppermute | solution.py:541
  14.1 5.7 %collective-permute-start.3 = (bf16[64,128]{1,0:T(8,128)(2,1)S(1)}, bf16[64,128]{1,0:T(8,128)(2,1)S(1)}, u32[]{:S(2)}, u32[]{:S(2)}) collective-permute-start(bf16[64,128]{1,0:T(8,128)(2,1)S(1)} %get-tuple-element.183), channel_id=1, source_target_pairs={{1,0},{2,1},{3,2},{4,3},{5,4},{6,5},{7,6},{8,7},{9,8},{10,9},{11,1... | collective-permute-start | bytes 49160 | tf_op jit(solution)/shard_map/ppermute | solution.py:542
  16.8 1.0 copy-start.1
  19.7 0.6 copy-start.14
  19.7 0.6 copy-start.15
  19.7 0.6 copy-start.16
  20.3 0.6 copy-start.17
  96.1 12.1 %copy-start.10 = (f32[5,64]{1,0:T(8,128)S(1)}, f32[5,64]{1,0:T(8,128)}, u32[]{:S(2)}) copy-start(f32[5,64]{1,0:T(8,128)} %gain_ref.1) | copy-start | bytes 3844
  96.1 12.2 %copy-start.5 = (bf16[2,256,64]{1,2,0:T(8,128)(2,1)S(1)}, bf16[2,256,64]{1,2,0:T(8,128)(2,1)}, u32[]{:S(2)}) copy-start(bf16[2,256,64]{1,2,0:T(8,128)(2,1)} %param.22) | copy-start | bytes 196612
  96.1 36.8 %copy-start.11 = (bf16[2,64,192]{2,1,0:T(8,128)(2,1)S(1)}, bf16[2,64,192]{2,1,0:T(8,128)(2,1)}, u32[]{:S(2)}) copy-start(bf16[2,64,192]{2,1,0:T(8,128)(2,1)} %qkv_ref.1) | copy-start | bytes 147460
  96.1 36.8 %copy-start.12 = (bf16[2,64,256]{2,1,0:T(8,128)(2,1)S(1)}, bf16[2,64,256]{2,1,0:T(8,128)(2,1)}, u32[]{:S(2)}) copy-start(bf16[2,64,256]{2,1,0:T(8,128)(2,1)} %up_ref.1) | copy-start | bytes 196612
  96.1 36.7 %copy-start.13 = (bf16[2,64,64]{2,1,0:T(8,128)(2,1)S(1)}, bf16[2,64,64]{2,1,0:T(8,128)(2,1)}, u32[]{:S(2)}) copy-start(bf16[2,64,64]{2,1,0:T(8,128)(2,1)} %outw_ref.1) | copy-start | bytes 49156
  96.1 30.8 %all-to-all-start.3 = ((bf16[128,32,128]{2,1,0:T(8,128)(2,1)}), bf16[128,32,128]{2,1,0:T(8,128)(2,1)S(1)}, u32[]{:S(2)}, u32[]{:S(2)}) async-start(bf16[128,32,128]{2,1,0:T(8,128)(2,1)} %bitcast.69), calls=%async_computation.3 | async-start | bytes 2097152 | tf_op jit(solution)/shard_map/all_to_all | solution.py:591
  127.0 1.0 copy-start
  182.1 29.6 %copy-start.2 = (s32[4096]{0:T(1024)S(1)}, s32[4096]{0:T(1024)}, u32[]{:S(2)}) copy-start(s32[4096]{0:T(1024)} %copy-done.1) | copy-start | bytes 49156
  182.1 29.6 %copy-start.7 = (s32[2,4096]{1,0:T(2,128)S(1)}, s32[2,4096]{1,0:T(2,128)}, u32[]{:S(2)}) copy-start(s32[2,4096]{1,0:T(2,128)} %param.17) | copy-start | bytes 98308
  182.1 29.6 %copy-start.9 = (s32[2,4096]{1,0:T(2,128)S(1)}, s32[2,4096]{1,0:T(2,128)}, u32[]{:S(2)}) copy-start(s32[2,4096]{1,0:T(2,128)} %param.16) | copy-start | bytes 98308
  182.1 27.1 %all-to-all-start.4 = ((bf16[128,40,128]{2,1,0:T(8,128)(2,1)}), bf16[128,40,128]{2,1,0:T(8,128)(2,1)}, u32[]{:S(2)}, u32[]{:S(2)}) async-start(bf16[128,40,128]{2,1,0:T(8,128)(2,1)} %bitcast.68), calls=%async_computation.4 | async-start | bytes 2621440 | tf_op jit(solution)/shard_map/all_to_all | solution.py:591
  254.0 0.8 copy-start.18
